TPU v7x, 256 devices: a whole 4x4x8 slice. The times are simulated.
256 devices in a mesh: tok: 32 (over x, z_hi, core), hid: 8 (over y, z_lo).
Axes of the slice: x: 4, y: 4, z: 8 (z_hi: 4, z_lo: 2; z = z_hi * 2 + z_lo), core: 2. Of those that a mesh axis runs over, the one named last changes fastest.
Arguments:
- base: float32 [1024, 16384], P('tok', 'hid'), may hold values from -6 to 6
- source: float32 [1024, 16384], P('tok', 'hid'), may hold values from -6 to 6
- pairs: int32 [1024], replicated, may hold values from 0 to 1023, each once
- counts: int32 [1024], replicated, may hold values from 1 to 128
- rotation: float32 [16384, 16384], P('hid', 'tok'), may hold values from -0.046875 to 0.046875
Outputs:
- patched: float32 [1024, 16384], P('tok', 'hid')
All inputs are finite; a program needn't handle non-finite values.
Results may differ from a plain program's by a relative error of at most 0.000075.
Values sent between devices are 32-bit elements; how exact they have to be, the bound alone decides.
No kernel may reach another device: no remote copies, remote signals or barrier semaphores. Data moves between devices by JAX's collectives and lax.ppermute only.
A program may use at most 64 MiB of HBM per device.

v0:
```python
import jax
import jax.numpy as jnp
from jax import lax
from jax.sharding import Mesh, PartitionSpec as P

BLOCK = 128
SIZES = {"x": 4, "zh": 4, "c": 2, "y": 4, "zl": 2}
HID = ("y", "zl")


def fetch(a, axis, d):
    n = SIZES[axis]
    return lax.ppermute(a, axis, [((i + d) % n, i) for i in range(n)])


def ring_gather(own, axis):
    half = own.shape[0] // 2
    ahead = fetch(own, axis, 1)
    behind = fetch(own, axis, -1)
    far = [fetch(ahead[:half], axis, 1), fetch(behind[half:], axis, -1)]
    return jnp.concatenate([own, ahead, *far, behind], axis=0)


def part(a, index, size):
    return lax.dynamic_slice_in_dim(a, index * size, size, 0)


def ring_scatter(terms, axis):
    me = lax.axis_index(axis)
    rows = terms.shape[0] // 4
    half = rows // 2
    own, ahead, far, behind = (part(terms, (me + d) % 4, rows) for d in range(4))
    to_ahead = fetch(far[:half], axis, -1)
    to_behind = fetch(far[half:], axis, 1)
    ahead = jnp.concatenate([ahead[:half] + to_ahead, ahead[half:]], axis=0)
    behind = jnp.concatenate([behind[:half], behind[half:] + to_behind], axis=0)
    return own + fetch(ahead, axis, -1) + fetch(behind, axis, 1)


def dot(a, b, dims):
    return lax.dot_general(
        a, b, (dims, ((), ())), precision=lax.Precision.HIGH, preferred_element_type=jnp.float32
    )


def local(base, source, pairs, counts, rotation):
    x, zh, c = (lax.axis_index(a) for a in ("x", "zh", "c"))
    features = rotation.shape[0] // 2
    width = rotation.shape[1]
    rows = base.shape[0]

    with jax.named_scope("core_swap_in"):
        both = jnp.concatenate([base, source], axis=0)
        mine = lax.dynamic_slice_in_dim(both, c * features, features, 1)
        theirs = fetch(lax.dynamic_slice_in_dim(both, (1 - c) * features, features, 1), "c", 1)
        first = jnp.where(c == 0, mine, theirs)
        second = jnp.where(c == 0, theirs, mine)
        matrix = jnp.concatenate(
            [part(rotation, c, features), fetch(part(rotation, 1 - c, features), "c", 1)], axis=1
        )

    with jax.named_scope("gather_base"):
        chip_base = jnp.concatenate([first[:rows], second[:rows]], axis=0)
        base_all = lax.all_gather(chip_base, ("x", "zh"), axis=0, tiled=True)

    with jax.named_scope("source_terms"):
        source_terms = jnp.concatenate(
            [
                dot(ring_gather(ring_gather(own, "zh"), "x"), matrix, ((1,), (0,)))
                for own in (first[rows:], second[rows:])
            ],
            axis=0,
        )

    with jax.named_scope("base_terms"):
        base_terms = dot(base_all, matrix, ((1,), (0,)))

    with jax.named_scope("select"):
        tok = (x * 4 + zh) * 2
        lane = jnp.arange(width, dtype=jnp.int32)
        columns = jnp.concatenate([(tok + c) * width + lane, (tok + 1 - c) * width + lane])
        spot = (
            (pairs // rows) % 2 * (16 * rows)
            + (pairs // 256 - x) % 4 * (4 * rows)
            + (pairs // 64 - zh) % 4 * rows
            + pairs % rows
        )
        taken = source_terms.at[spot].get(mode="promise_in_bounds")
        mixed = jnp.where(columns[None, :] < (counts * BLOCK)[:, None], taken, base_terms)

    with jax.named_scope("reduce_hid"):
        mixed = mixed[:, :width] + fetch(mixed[:, width:], "c", 1)
        share = mixed.shape[0] // 8
        mixed = lax.all_to_all(mixed.reshape(8, share, width), HID, 0, 0)
        mixed = mixed.sum(axis=0)
    with jax.named_scope("gather_hid"):
        full = lax.all_to_all(jnp.broadcast_to(mixed, (8, share, width)), HID, 0, 0)
        full = full.reshape(8 * share, width)
        other = fetch(full, "c", 1)

    with jax.named_scope("inverse"):
        terms = dot(jnp.concatenate([full, other], axis=1), matrix, ((1,), (1,)))
    with jax.named_scope("scatter"):
        out = ring_scatter(ring_scatter(terms, "x"), "zh")

    with jax.named_scope("core_swap_out"):
        mine = part(out, c, rows)
        theirs = fetch(part(out, 1 - c, rows), "c", 1)
        return jnp.where(
            c == 0,
            jnp.concatenate([mine, theirs], axis=1),
            jnp.concatenate([theirs, mine], axis=1),
        )


def solution(mesh):
    fine = Mesh(mesh.devices.reshape(4, 4, 2, 4, 2), ("x", "zh", "c", "y", "zl"))
    tok = ("x", "zh", "c")
    return jax.shard_map(
        local,
        mesh=fine,
        in_specs=(P(tok, HID), P(tok, HID), P(), P(), P(HID, tok)),
        out_specs=P(tok, HID),
        check_vma=False,
    )
```

profile of v0, /device:TPU:1, one launch (start us, length us, event | category | flops | bytes accessed | tf_op | source)
XLA Modules:
  0.0 305.9 jit_solution(6457067190570654591)
XLA Ops:
  15.3 4.4 %collective-permute-start.1 = (f32[32,1024]{1,0:T(8,128)S(1)}, f32[32,1024]{1,0:T(8,128)S(1)}, u32[]{:S(2)}, u32[]{:S(2)}) collective-permute-start(f32[32,1024]{1,0:T(8,128)S(1)} %get-tuple-element.26), channel_id=1, source_target_pairs={{16,0},{32,16},{48,32},{0,48},{17,1},{33,17},{49,33},{1,49},{18,2}... | collective-permute-start | bytes 393224 | tf_op jit(solution)/shard_map/source_terms/ppermute | solution.py:13
  23.2 4.0 %constant_dynamic-slice_fusion.11 = (f32[1024,512]{1,0:T(8,128)S(1)}, f32[1024,512]{1,0:T(8,128)}) fusion(f32[2048,512]{1,0:T(8,128)} %param.9, s32[]{:T(128)S(6)} %select_n.131, s32[]{:T(128)S(6)} %select_n.132), kind=kLoop, calls=%fused_computation.88 | loop fusion | bytes 8388616 | tf_op jit(solution)/shard_map/core_swap_in/dynamic_slice | solution.py:25
  28.5 3.9 %collective-permute-start.2 = (f32[16,1024]{1,0:T(8,128)S(1)}, f32[16,1024]{1,0:T(8,128)S(1)}, u32[]{:S(2)}, u32[]{:S(2)}) collective-permute-start(f32[16,1024]{1,0:T(8,128)S(1)} %slice.107), channel_id=1, source_target_pairs={{16,0},{32,16},{48,32},{0,48},{17,1},{33,17},{49,33},{1,49},{18,2}... | collective-permute-start | bytes 196616 | tf_op jit(solution)/shard_map/source_terms/ppermute | solution.py:13
  32.5 3.6 %collective-permute-start.11 = (f32[16,1024]{1,0:T(8,128)S(1)}, f32[16,1024]{1,0:T(8,128)S(1)}, u32[]{:S(2)}, u32[]{:S(2)}) collective-permute-start(f32[16,1024]{1,0:T(8,128)S(1)} %slice.112), channel_id=1, source_target_pairs={{16,0},{32,16},{48,32},{0,48},{17,1},{33,17},{49,33},{1,49},{18,2}... | collective-permute-start | bytes 196616 | tf_op jit(solution)/shard_map/source_terms/ppermute | solution.py:13
  38.3 3.6 %collective-permute-done.4 = f32[16,1024]{1,0:T(8,128)S(1)} collective-permute-done((f32[16,1024]{1,0:T(8,128)S(1)}, f32[16,1024]{1,0:T(8,128)S(1)}, u32[]{:S(2)}, u32[]{:S(2)}) %collective-permute-start.4) | collective-permute-done | bytes 65568 | tf_op jit(solution)/shard_map/source_terms/ppermute | solution.py:13
  50.8 6.7 %collective-permute-done.5 = f32[128,1024]{1,0:T(8,128)S(1)} collective-permute-done((f32[128,1024]{1,0:T(8,128)S(1)}, f32[128,1024]{1,0:T(8,128)S(1)}, u32[]{:S(2)}, u32[]{:S(2)}) %collective-permute-start.5) | collective-permute-done | bytes 524320 | tf_op jit(solution)/shard_map/source_terms/ppermute | solution.py:13
  57.5 3.7 %collective-permute-start.6 = (f32[64,1024]{1,0:T(8,128)S(1)}, f32[64,1024]{1,0:T(8,128)S(1)}, u32[]{:S(2)}, u32[]{:S(2)}) collective-permute-start(f32[64,1024]{1,0:T(8,128)S(1)} %slice.109), channel_id=1, source_target_pairs={{64,0},{128,64},{192,128},{0,192},{65,1},{129,65},{193,129},{1,193... | collective-permute-start | bytes 786440 | tf_op jit(solution)/shard_map/source_terms/ppermute | solution.py:13
  61.4 16.3 %collective-permute-done.14 = f32[128,1024]{1,0:T(8,128)S(1)} collective-permute-done((f32[128,1024]{1,0:T(8,128)}, f32[128,1024]{1,0:T(8,128)S(1)}, u32[]{:S(2)}, u32[]{:S(2)}) %collective-permute-start.14) | collective-permute-done | bytes 524320 | tf_op jit(solution)/shard_map/source_terms/ppermute | solution.py:13
  82.2 6.6 %collective-permute-done.6 = f32[64,1024]{1,0:T(8,128)S(1)} collective-permute-done((f32[64,1024]{1,0:T(8,128)S(1)}, f32[64,1024]{1,0:T(8,128)S(1)}, u32[]{:S(2)}, u32[]{:S(2)}) %collective-permute-start.6) | collective-permute-done | bytes 262176 | tf_op jit(solution)/shard_map/source_terms/ppermute | solution.py:13
  90.7 6.1 %collective-permute-done.15 = f32[64,1024]{1,0:T(8,128)S(1)} collective-permute-done((f32[64,1024]{1,0:T(8,128)S(1)}, f32[64,1024]{1,0:T(8,128)S(1)}, u32[]{:S(2)}, u32[]{:S(2)}) %collective-permute-start.15) | collective-permute-done | bytes 262176 | tf_op jit(solution)/shard_map/source_terms/ppermute | solution.py:13
  101.0 5.3 %fusion.6 = f32[512,1024]{1,0:T(8,128)S(1)} fusion(f32[512,1024]{1,0:T(8,128)S(1)} %constant_dynamic-update-slice_fusion.7, f32[1024,512]{1,0:T(8,128)} %collective-permute-done.9, f32[1024,512]{1,0:T(8,128)S(1)} %get-tuple-element.11), kind=kOutput, calls=%fused_computation.11 | convolution fusion | flops 3222274048 | bytes 8388608 | tf_op jit(solution)/shard_map/source_terms/dot_general | solution.py:41
  106.3 5.1 %fusion.5 = f32[512,1024]{1,0:T(8,128)S(1)} fusion(f32[512,1024]{1,0:T(8,128)S(1)} %copy-done.3, f32[1024,512]{1,0:T(8,128)} %collective-permute-done.9, f32[1024,512]{1,0:T(8,128)S(1)} %get-tuple-element.11), kind=kOutput, calls=%fused_computation.10 | convolution fusion | flops 3222274048 | bytes 8388608 | tf_op jit(solution)/shard_map/source_terms/dot_general | solution.py:41
  114.0 8.6 %gather_fusion = f32[1024,1024]{1,0:T(8,128)} fusion(f32[1024,1024]{1,0:T(8,128)} %pad_maximum_fusion.1, s32[1024]{0:T(1024)S(1)} %get-tuple-element.47), kind=kCustom, calls=%fused_computation | custom fusion | bytes 8392704 | tf_op jit(solution)/shard_map/select/gather | solution.py:88
  122.7 9.5 %fusion.4 = f32[1024,1024]{1,0:T(8,128)S(1)} fusion(f32[1024,1024]{1,0:T(8,128)} %all-gather.2.cloned.1.call-done, f32[1024,512]{1,0:T(8,128)} %collective-permute-done.9, f32[1024,512]{1,0:T(8,128)S(1)} %get-tuple-element.11), kind=kOutput, calls=%fused_computation.9 | convolution fusion | flops 6443499520 | bytes 12582912 | tf_op jit(solution)/shard_map/base_terms/dot_general | solution.py:41
  132.9 11.1 %collective-permute-start.18 = (f32[1024,512]{1,0:T(8,128)S(1)}, f32[1024,512]{1,0:T(8,128)S(1)}, u32[]{:S(2)}, u32[]{:S(2)}) collective-permute-start(f32[1024,512]{1,0:T(8,128)S(1)} %slice.119), channel_id=1, source_target_pairs={{8,0},{0,8},{9,1},{1,9},{10,2},{2,10},{11,3},{3,11},{12,4},{4,12},... | collective-permute-start | bytes 6291464 | tf_op jit(solution)/shard_map/reduce_hid/ppermute | solution.py:13
  144.0 3.8 %collective-permute-done.18 = f32[1024,512]{1,0:T(8,128)S(1)} collective-permute-done((f32[1024,512]{1,0:T(8,128)S(1)}, f32[1024,512]{1,0:T(8,128)S(1)}, u32[]{:S(2)}, u32[]{:S(2)}) %collective-permute-start.18) | collective-permute-done | bytes 2097184 | tf_op jit(solution)/shard_map/reduce_hid/ppermute | solution.py:13
  148.3 31.8 %all_to_all.10 = f32[8,128,512]{2,1,0:T(8,128)} all-to-all(f32[8,128,512]{2,1,0:T(8,128)S(1)} %bitcast.5), channel_id=1, replica_groups=mesh['x'=4,'zh'=4,'c'=2,'y'=4,'zl'=2] {'y','zl'}, dimensions={0} | all-to-all | bytes 4194304 | tf_op jit(solution)/shard_map/reduce_hid/all_to_all | solution.py:94
  182.1 28.3 %all_to_all.11 = f32[8,128,512]{2,1,0:T(8,128)} all-to-all(f32[8,128,512]{2,1,0:T(8,128)S(1)} %broadcast_in_dim.9), channel_id=1, replica_groups=mesh['x'=4,'zh'=4,'c'=2,'y'=4,'zl'=2] {'y','zl'}, dimensions={0} | all-to-all | bytes 4194304 | tf_op jit(solution)/shard_map/gather_hid/all_to_all | solution.py:97
  213.2 4.1 %collective-permute-done.19 = f32[1024,512]{1,0:T(8,128)} collective-permute-done((f32[1024,512]{1,0:T(8,128)}, f32[1024,512]{1,0:T(8,128)}, u32[]{:S(2)}, u32[]{:S(2)}) %collective-permute-start.19) | collective-permute-done | bytes 2097184 | tf_op jit(solution)/shard_map/gather_hid/ppermute | solution.py:13
  217.3 9.3 %fusion = f32[1024,1024]{1,0:T(8,128)S(1)} fusion(f32[1024,512]{1,0:T(8,128)} %collective-permute-done.19, f32[1024,512]{1,0:T(8,128)} %bitcast.1, f32[1024,512]{1,0:T(8,128)} %collective-permute-done.9, f32[1024,512]{1,0:T(8,128)S(1)} %get-tuple-element.11), kind=kOutput, calls=%fused_computation.3 | convolution fusion | flops 6444548096 | bytes 12582912 | tf_op jit(solution)/shard_map/inverse/dot_general | solution.py:41
  231.4 11.7 %collective-permute-done.20 = f32[128,1024]{1,0:T(8,128)S(1)} collective-permute-done((f32[128,1024]{1,0:T(8,128)S(1)}, f32[128,1024]{1,0:T(8,128)S(1)}, u32[]{:S(2)}, u32[]{:S(2)}) %collective-permute-start.20) | collective-permute-done | bytes 524320 | tf_op jit(solution)/shard_map/scatter/ppermute | solution.py:13
  248.8 20.9 %collective-permute-done.21 = f32[256,1024]{1,0:T(8,128)S(1)} collective-permute-done((f32[256,1024]{1,0:T(8,128)S(1)}, f32[256,1024]{1,0:T(8,128)S(1)}, u32[]{:S(2)}, u32[]{:S(2)}) %collective-permute-start.21) | collective-permute-done | bytes 1048608 | tf_op jit(solution)/shard_map/scatter/ppermute | solution.py:13
  275.2 5.1 %collective-permute-done.24 = f32[32,1024]{1,0:T(8,128)S(1)} collective-permute-done((f32[32,1024]{1,0:T(8,128)S(1)}, f32[32,1024]{1,0:T(8,128)S(1)}, u32[]{:S(2)}, u32[]{:S(2)}) %collective-permute-start.24) | collective-permute-done | bytes 131104 | tf_op jit(solution)/shard_map/scatter/ppermute | solution.py:13
  284.1 9.5 %collective-permute-done.25 = f32[64,1024]{1,0:T(8,128)S(1)} collective-permute-done((f32[64,1024]{1,0:T(8,128)S(1)}, f32[64,1024]{1,0:T(8,128)S(1)}, u32[]{:S(2)}, u32[]{:S(2)}) %collective-permute-start.25) | collective-permute-done | bytes 262176 | tf_op jit(solution)/shard_map/scatter/ppermute | solution.py:13
  (110 shorter events, 68.8 us)
Async XLA Ops:
  6.5 116.1 %all-gather.2.cloned.1.call-start = ((), (), s32[]{:S(2)}) async-start(), calls=%async_computation.2 | async-start | bytes 4456448 | tf_op jit(solution)/shard_map/gather_base/all_gather | solution.py:64
  15.3 13.2 %collective-permute-start.1 = (f32[32,1024]{1,0:T(8,128)S(1)}, f32[32,1024]{1,0:T(8,128)S(1)}, u32[]{:S(2)}, u32[]{:S(2)}) collective-permute-start(f32[32,1024]{1,0:T(8,128)S(1)} %get-tuple-element.26), channel_id=1, source_target_pairs={{16,0},{32,16},{48,32},{0,48},{17,1},{33,17},{49,33},{1,49},{18,2}... | collective-permute-start | bytes 393224 | tf_op jit(solution)/shard_map/source_terms/ppermute | solution.py:13
  19.6 12.8 %collective-permute-start.3 = (f32[32,1024]{1,0:T(8,128)S(1)}, f32[32,1024]{1,0:T(8,128)S(1)}, u32[]{:S(2)}, u32[]{:S(2)}) collective-permute-start(f32[32,1024]{1,0:T(8,128)S(1)} %get-tuple-element.26), channel_id=1, source_target_pairs={{48,0},{0,16},{16,32},{32,48},{49,1},{1,17},{17,33},{33,49},{50,2}... | collective-permute-start | bytes 393224 | tf_op jit(solution)/shard_map/source_terms/ppermute | solution.py:13
  19.6 12.9 %collective-permute-start.10 = (f32[32,1024]{1,0:T(8,128)S(1)}, f32[32,1024]{1,0:T(8,128)S(1)}, u32[]{:S(2)}, u32[]{:S(2)}) collective-permute-start(f32[32,1024]{1,0:T(8,128)S(1)} %get-tuple-element.30), channel_id=1, source_target_pairs={{16,0},{32,16},{48,32},{0,48},{17,1},{33,17},{49,33},{1,49},{18,2}... | collective-permute-start | bytes 393224 | tf_op jit(solution)/shard_map/source_terms/ppermute | solution.py:13
  23.2 12.9 %collective-permute-start.12 = (f32[32,1024]{1,0:T(8,128)S(1)}, f32[32,1024]{1,0:T(8,128)S(1)}, u32[]{:S(2)}, u32[]{:S(2)}) collective-permute-start(f32[32,1024]{1,0:T(8,128)S(1)} %get-tuple-element.30), channel_id=1, source_target_pairs={{48,0},{0,16},{16,32},{32,48},{49,1},{1,17},{17,33},{33,49},{50,2}... | collective-permute-start | bytes 393224 | tf_op jit(solution)/shard_map/source_terms/ppermute | solution.py:13
  27.2 73.8 %collective-permute-start.9 = (f32[1024,512]{1,0:T(8,128)}, f32[1024,512]{1,0:T(8,128)}, u32[]{:S(2)}, u32[]{:S(2)}) collective-permute-start(f32[1024,512]{1,0:T(8,128)} %get-tuple-element.12), channel_id=1, source_target_pairs={{8,0},{0,8},{9,1},{1,9},{10,2},{2,10},{11,3},{3,11},{12,4},{4,12},... | collective-permute-start | bytes 6291464 | tf_op jit(solution)/shard_map/core_swap_in/ppermute | solution.py:13
  32.4 9.5 %collective-permute-start.4 = (f32[16,1024]{1,0:T(8,128)S(1)}, f32[16,1024]{1,0:T(8,128)S(1)}, u32[]{:S(2)}, u32[]{:S(2)}) collective-permute-start(f32[16,1024]{1,0:T(8,128)S(1)} %slice.108), channel_id=1, source_target_pairs={{48,0},{0,16},{16,32},{32,48},{49,1},{1,17},{17,33},{33,49},{50,2}... | collective-permute-start | bytes 196616 | tf_op jit(solution)/shard_map/source_terms/ppermute | solution.py:13
  32.5 13.5 %collective-permute-start.11 = (f32[16,1024]{1,0:T(8,128)S(1)}, f32[16,1024]{1,0:T(8,128)S(1)}, u32[]{:S(2)}, u32[]{:S(2)}) collective-permute-start(f32[16,1024]{1,0:T(8,128)S(1)} %slice.112), channel_id=1, source_target_pairs={{16,0},{32,16},{48,32},{0,48},{17,1},{33,17},{49,33},{1,49},{18,2}... | collective-permute-start | bytes 196616 | tf_op jit(solution)/shard_map/source_terms/ppermute | solution.py:13
  36.2 10.5 %collective-permute-start.13 = (f32[16,1024]{1,0:T(8,128)S(1)}, f32[16,1024]{1,0:T(8,128)S(1)}, u32[]{:S(2)}, u32[]{:S(2)}) collective-permute-start(f32[16,1024]{1,0:T(8,128)S(1)} %slice.113), channel_id=1, source_target_pairs={{48,0},{0,16},{16,32},{32,48},{49,1},{1,17},{17,33},{33,49},{50,2}... | collective-permute-start | bytes 196616 | tf_op jit(solution)/shard_map/source_terms/ppermute | solution.py:13
  43.2 14.3 %collective-permute-start.5 = (f32[128,1024]{1,0:T(8,128)S(1)}, f32[128,1024]{1,0:T(8,128)S(1)}, u32[]{:S(2)}, u32[]{:S(2)}) collective-permute-start(f32[128,1024]{1,0:T(8,128)S(1)} %get-tuple-element.31), channel_id=1, source_target_pairs={{64,0},{128,64},{192,128},{0,192},{65,1},{129,65},{193,129},{1,193... | collective-permute-start | bytes 1572872 | tf_op jit(solution)/shard_map/source_terms/ppermute | solution.py:13
  46.0 15.3 %collective-permute-start.7 = (f32[128,1024]{1,0:T(8,128)S(1)}, f32[128,1024]{1,0:T(8,128)S(1)}, u32[]{:S(2)}, u32[]{:S(2)}) collective-permute-start(f32[128,1024]{1,0:T(8,128)S(1)} %get-tuple-element.31), channel_id=1, source_target_pairs={{192,0},{0,64},{64,128},{128,192},{193,1},{1,65},{65,129},{129,193... | collective-permute-start | bytes 1572872 | tf_op jit(solution)/shard_map/source_terms/ppermute | solution.py:13
  48.0 29.6 %collective-permute-start.14 = (f32[128,1024]{1,0:T(8,128)}, f32[128,1024]{1,0:T(8,128)S(1)}, u32[]{:S(2)}, u32[]{:S(2)}) collective-permute-start(f32[128,1024]{1,0:T(8,128)} %get-tuple-element.35), channel_id=1, source_target_pairs={{64,0},{128,64},{192,128},{0,192},{65,1},{129,65},{193,129},{1,193... | collective-permute-start | bytes 1572872 | tf_op jit(solution)/shard_map/source_terms/ppermute | solution.py:13
  50.7 30.5 %collective-permute-start.16 = (f32[128,1024]{1,0:T(8,128)}, f32[128,1024]{1,0:T(8,128)S(1)}, u32[]{:S(2)}, u32[]{:S(2)}) collective-permute-start(f32[128,1024]{1,0:T(8,128)} %get-tuple-element.35), channel_id=1, source_target_pairs={{192,0},{0,64},{64,128},{128,192},{193,1},{1,65},{65,129},{129,193... | collective-permute-start | bytes 1572872 | tf_op jit(solution)/shard_map/source_terms/ppermute | solution.py:13
  57.5 31.3 %collective-permute-start.6 = (f32[64,1024]{1,0:T(8,128)S(1)}, f32[64,1024]{1,0:T(8,128)S(1)}, u32[]{:S(2)}, u32[]{:S(2)}) collective-permute-start(f32[64,1024]{1,0:T(8,128)S(1)} %slice.109), channel_id=1, source_target_pairs={{64,0},{128,64},{192,128},{0,192},{65,1},{129,65},{193,129},{1,193... | collective-permute-start | bytes 786440 | tf_op jit(solution)/shard_map/source_terms/ppermute | solution.py:13
  61.3 29.4 %collective-permute-start.8 = (f32[64,1024]{1,0:T(8,128)S(1)}, f32[64,1024]{1,0:T(8,128)S(1)}, u32[]{:S(2)}, u32[]{:S(2)}) collective-permute-start(f32[64,1024]{1,0:T(8,128)S(1)} %slice.110), channel_id=1, source_target_pairs={{192,0},{0,64},{64,128},{128,192},{193,1},{1,65},{65,129},{129,193... | collective-permute-start | bytes 786440 | tf_op jit(solution)/shard_map/source_terms/ppermute | solution.py:13
  77.7 19.1 %collective-permute-start.15 = (f32[64,1024]{1,0:T(8,128)S(1)}, f32[64,1024]{1,0:T(8,128)S(1)}, u32[]{:S(2)}, u32[]{:S(2)}) collective-permute-start(f32[64,1024]{1,0:T(8,128)S(1)} %slice.114), channel_id=1, source_target_pairs={{64,0},{128,64},{192,128},{0,192},{65,1},{129,65},{193,129},{1,193... | collective-permute-start | bytes 786440 | tf_op jit(solution)/shard_map/source_terms/ppermute | solution.py:13
  81.2 18.1 %collective-permute-start.17 = (f32[64,1024]{1,0:T(8,128)S(1)}, f32[64,1024]{1,0:T(8,128)S(1)}, u32[]{:S(2)}, u32[]{:S(2)}) collective-permute-start(f32[64,1024]{1,0:T(8,128)S(1)} %slice.115), channel_id=1, source_target_pairs={{192,0},{0,64},{64,128},{128,192},{193,1},{1,65},{65,129},{129,193... | collective-permute-start | bytes 786440 | tf_op jit(solution)/shard_map/source_terms/ppermute | solution.py:13
  132.9 14.9 %collective-permute-start.18 = (f32[1024,512]{1,0:T(8,128)S(1)}, f32[1024,512]{1,0:T(8,128)S(1)}, u32[]{:S(2)}, u32[]{:S(2)}) collective-permute-start(f32[1024,512]{1,0:T(8,128)S(1)} %slice.119), channel_id=1, source_target_pairs={{8,0},{0,8},{9,1},{1,9},{10,2},{2,10},{11,3},{3,11},{12,4},{4,12},... | collective-permute-start | bytes 6291464 | tf_op jit(solution)/shard_map/reduce_hid/ppermute | solution.py:13
  228.7 14.4 %collective-permute-start.20 = (f32[128,1024]{1,0:T(8,128)S(1)}, f32[128,1024]{1,0:T(8,128)S(1)}, u32[]{:S(2)}, u32[]{:S(2)}) collective-permute-start(f32[128,1024]{1,0:T(8,128)S(1)} %get-tuple-element.9), channel_id=1, source_target_pairs={{192,0},{0,64},{64,128},{128,192},{193,1},{1,65},{65,129},{129,193... | collective-permute-start | bytes 1572872 | tf_op jit(solution)/shard_map/scatter/ppermute | solution.py:13
  228.8 14.3 %collective-permute-start.22 = (f32[128,1024]{1,0:T(8,128)S(1)}, f32[128,1024]{1,0:T(8,128)S(1)}, u32[]{:S(2)}, u32[]{:S(2)}) collective-permute-start(f32[128,1024]{1,0:T(8,128)S(1)} %get-tuple-element.10), channel_id=1, source_target_pairs={{64,0},{128,64},{192,128},{0,192},{65,1},{129,65},{193,129},{1,193... | collective-permute-start | bytes 1572872 | tf_op jit(solution)/shard_map/scatter/ppermute | solution.py:13
  244.9 24.7 %collective-permute-start.21 = (f32[256,1024]{1,0:T(8,128)S(1)}, f32[256,1024]{1,0:T(8,128)S(1)}, u32[]{:S(2)}, u32[]{:S(2)}) collective-permute-start(f32[256,1024]{1,0:T(8,128)S(1)} %pad_maximum_fusion.6), channel_id=1, source_target_pairs={{192,0},{0,64},{64,128},{128,192},{193,1},{1,65},{65,129},{129,193... | collective-permute-start | bytes 3145736 | tf_op jit(solution)/shard_map/scatter/ppermute | solution.py:13
  246.1 23.9 %collective-permute-start.23 = (f32[256,1024]{1,0:T(8,128)}, f32[256,1024]{1,0:T(8,128)S(1)}, u32[]{:S(2)}, u32[]{:S(2)}) collective-permute-start(f32[256,1024]{1,0:T(8,128)} %pad_maximum_fusion.7), channel_id=1, source_target_pairs={{64,0},{128,64},{192,128},{0,192},{65,1},{129,65},{193,129},{1,193... | collective-permute-start | bytes 3145736 | tf_op jit(solution)/shard_map/scatter/ppermute | solution.py:13
  280.4 13.3 %collective-permute-start.25 = (f32[64,1024]{1,0:T(8,128)S(1)}, f32[64,1024]{1,0:T(8,128)S(1)}, u32[]{:S(2)}, u32[]{:S(2)}) collective-permute-start(f32[64,1024]{1,0:T(8,128)S(1)} %pad_maximum_fusion.9), channel_id=1, source_target_pairs={{48,0},{0,16},{16,32},{32,48},{49,1},{1,17},{17,33},{33,49},{50,2}... | collective-permute-start | bytes 786440 | tf_op jit(solution)/shard_map/scatter/ppermute | solution.py:13
  281.6 12.1 %collective-permute-start.27 = (f32[64,1024]{1,0:T(8,128)S(1)}, f32[64,1024]{1,0:T(8,128)S(1)}, u32[]{:S(2)}, u32[]{:S(2)}) collective-permute-start(f32[64,1024]{1,0:T(8,128)S(1)} %pad_maximum_fusion.10), channel_id=1, source_target_pairs={{16,0},{32,16},{48,32},{0,48},{17,1},{33,17},{49,33},{1,49},{18,2}... | collective-permute-start | bytes 786440 | tf_op jit(solution)/shard_map/scatter/ppermute | solution.py:13
  (12 other events, 154.7 us)
Sparse Core Ops, SparseCore 0:
  15.4 81.8 all-gather.1
where the time goes:
time: 310 us; the launch traced here: 306 us
  waiting for transfers between devices  101 us (33%)
  starting transfers between devices  63.2 us (20%)
  blocking collectives  60.1 us (19%)
  matrix products  29.2 us (9%)
  local copies, waits for them, and re-layouts  27.4 us (9%)
  between operations  13.9 us (4%)
  other arithmetic  11.5 us (4%)
    ppermute x29, waiting for transfers between devices, fetch(): return lax.ppermute(a, axis, [((i + d) % n, i) for i in range(n)])  101 us
    ppermute x29, starting transfers between devices, fetch(): return lax.ppermute(a, axis, [((i + d) % n, i) for i in range(n)])  63.2 us
    all_to_all x1, blocking collectives, local(): mixed = lax.all_to_all(mixed.reshape(8, share, width), HID, 0, 0)  31.8 us
    dot_general x4, matrix products, dot(): lax.dot_general(a, b, (dims, ((), ())), precision=lax.Precision.HIGH, pre...  29.2 us
    all_to_all x1, blocking collectives, local(): full = lax.all_to_all(jnp.broadcast_to(mixed, (8, share, width)), HID, 0, 0)  28.3 us
    unnamed x25, local copies, waits for them, and re-layouts  9.36 us
    gather x1, local copies, waits for them, and re-layouts, local(): taken = source_terms.at[spot].get(mode='promise_in_bounds')  8.61 us
  transfers between devices with their start and end apart: 30, of which 16 were waited for; matrix products, arithmetic and copies ran while one was open for 12% of the time, Pallas kernels for 0%

commit v1 on v0

--- a/solution.py
+++ b/solution.py
@@ -6,6 +6,7 @@
 BLOCK = 128
 SIZES = {"x": 4, "zh": 4, "c": 2, "y": 4, "zl": 2}
 HID = ("y", "zl")
+RING = 640
 
 
 def fetch(a, axis, d):
@@ -51,10 +52,14 @@
 
     with jax.named_scope("core_swap_in"):
         both = jnp.concatenate([base, source], axis=0)
-        mine = lax.dynamic_slice_in_dim(both, c * features, features, 1)
-        theirs = fetch(lax.dynamic_slice_in_dim(both, (1 - c) * features, features, 1), "c", 1)
+        low, high = both[:, :features], both[:, features:]
+        mine = jnp.where(c == 0, low, high)
+        theirs = fetch(jnp.where(c == 0, high, low), "c", 1)
         first = jnp.where(c == 0, mine, theirs)
         second = jnp.where(c == 0, theirs, mine)
+        first, second, pairs, counts, rotation = lax.optimization_barrier(
+            (first, second, pairs, counts, rotation)
+        )
         matrix = jnp.concatenate(
             [part(rotation, c, features), fetch(part(rotation, 1 - c, features), "c", 1)], axis=1
         )
@@ -99,9 +104,13 @@
         other = fetch(full, "c", 1)
 
     with jax.named_scope("inverse"):
-        terms = dot(jnp.concatenate([full, other], axis=1), matrix, ((1,), (1,)))
+        full = jnp.concatenate([full, other], axis=1)
+        last = dot(full, matrix[RING:], ((1,), (1,)))
+        terms = dot(full, matrix[:RING], ((1,), (1,)))
     with jax.named_scope("scatter"):
+        last = lax.psum_scatter(last, ("x", "zh"), scatter_dimension=0, tiled=True)
         out = ring_scatter(ring_scatter(terms, "x"), "zh")
+        out = jnp.concatenate([out, last], axis=1)
 
     with jax.named_scope("core_swap_out"):
         mine = part(out, c, rows)

time: 310 us -> 327 us (1.055)
  local copies, waits for them, and re-layouts: 27.4 us -> 34.7 us
  matrix products: 29.2 us -> 35.5 us
  waiting for transfers between devices: 101 us -> 107 us
    reduce_scatter x0 -> x1, waiting for transfers between devices: none -> 22.8 us  [local(): last = lax.psum_scatter(last, ('x', 'zh'), scatter_dimension=0, tiled=True)]
    ppermute x29, waiting for transfers between devices: 101 us -> 84.1 us  [fetch(): return lax.ppermute(a, axis, [((i + d) % n, i) for i in range(n)])]
    dot_general x4 -> x5, matrix products: 29.2 us -> 35.5 us  [dot(): lax.dot_general(a, b, (dims, ((), ())), precision=lax.Precision.HIGH, pre...]
    unnamed x25, local copies, waits for them, and re-layouts: 9.36 us -> 13 us
  transfers between devices with their start and end apart: 30 -> 31, of which waited for: 16 -> 17; matrix products, arithmetic and copies ran while one was open for 12% -> 16% of each run, Pallas kernels for 0% -> 0%
where the time goes in v1:
time: 327 us; the launch traced here: 322 us
  waiting for transfers between devices  107 us (33%)
  blocking collectives  60.4 us (18%)
  starting transfers between devices  60 us (18%)
  matrix products  35.5 us (11%)
  local copies, waits for them, and re-layouts  34.7 us (11%)
  between operations  13.9 us (4%)
  other arithmetic  10.5 us (3%)
    ppermute x29, waiting for transfers between devices, fetch(): return lax.ppermute(a, axis, [((i + d) % n, i) for i in range(n)])  84.1 us
    ppermute x29, starting transfers between devices, fetch(): return lax.ppermute(a, axis, [((i + d) % n, i) for i in range(n)])  60 us
    dot_general x5, matrix products, dot(): lax.dot_general(a, b, (dims, ((), ())), precision=lax.Precision.HIGH, pre...  35.5 us
    all_to_all x1, blocking collectives, local(): mixed = lax.all_to_all(mixed.reshape(8, share, width), HID, 0, 0)  32.1 us
    all_to_all x1, blocking collectives, local(): full = lax.all_to_all(jnp.broadcast_to(mixed, (8, share, width)), HID, 0, 0)  28.3 us
    reduce_scatter x1, waiting for transfers between devices, local(): last = lax.psum_scatter(last, ('x', 'zh'), scatter_dimension=0, tiled=True)  22.8 us
    unnamed x25, local copies, waits for them, and re-layouts  13 us
    gather x1, local copies, waits for them, and re-layouts, local(): taken = source_terms.at[spot].get(mode='promise_in_bounds')  8.6 us
  transfers between devices with their start and end apart: 31, of which 17 were waited for; matrix products, arithmetic and copies ran while one was open for 16% of the time, Pallas kernels for 0%

profile of v1, /device:TPU:1, one launch (start us, length us, event | category | flops | bytes accessed | tf_op | source)
XLA Modules:
  0.0 322.0 jit_solution(2351502436818418803)
XLA Ops:
  15.3 4.4 %collective-permute-start.1 = (f32[32,1024]{1,0:T(8,128)S(1)}, f32[32,1024]{1,0:T(8,128)S(1)}, u32[]{:S(2)}, u32[]{:S(2)}) collective-permute-start(f32[32,1024]{1,0:T(8,128)S(1)} %get-tuple-element.36), channel_id=1, source_target_pairs={{16,0},{32,16},{48,32},{0,48},{17,1},{33,17},{49,33},{1,49},{18,2}... | collective-permute-start | bytes 393224 | tf_op jit(solution)/shard_map/source_terms/ppermute | solution.py:14
  23.3 4.0 %constant_dynamic-slice_fusion.9 = (f32[1024,512]{1,0:T(8,128)S(1)}, f32[1024,512]{1,0:T(8,128)}) fusion(f32[2048,512]{1,0:T(8,128)} %param.9, s32[]{:T(128)S(6)} %select_n.141, s32[]{:T(128)S(6)} %select_n.142), kind=kLoop, calls=%fused_computation.99 | loop fusion | bytes 8388616 | tf_op jit(solution)/shard_map/core_swap_in/dynamic_slice | solution.py:26
  28.5 3.9 %collective-permute-start.2 = (f32[16,1024]{1,0:T(8,128)S(1)}, f32[16,1024]{1,0:T(8,128)S(1)}, u32[]{:S(2)}, u32[]{:S(2)}) collective-permute-start(f32[16,1024]{1,0:T(8,128)S(1)} %slice.124), channel_id=1, source_target_pairs={{16,0},{32,16},{48,32},{0,48},{17,1},{33,17},{49,33},{1,49},{18,2}... | collective-permute-start | bytes 196616 | tf_op jit(solution)/shard_map/source_terms/ppermute | solution.py:14
  38.3 3.7 %collective-permute-done.4 = f32[16,1024]{1,0:T(8,128)S(1)} collective-permute-done((f32[16,1024]{1,0:T(8,128)S(1)}, f32[16,1024]{1,0:T(8,128)S(1)}, u32[]{:S(2)}, u32[]{:S(2)}) %collective-permute-start.4) | collective-permute-done | bytes 65568 | tf_op jit(solution)/shard_map/source_terms/ppermute | solution.py:14
  51.7 6.8 %collective-permute-done.5 = f32[128,1024]{1,0:T(8,128)S(1)} collective-permute-done((f32[128,1024]{1,0:T(8,128)}, f32[128,1024]{1,0:T(8,128)S(1)}, u32[]{:S(2)}, u32[]{:S(2)}) %collective-permute-start.5) | collective-permute-done | bytes 524320 | tf_op jit(solution)/shard_map/source_terms/ppermute | solution.py:14
  60.4 17.0 %collective-permute-done.14 = f32[128,1024]{1,0:T(8,128)} collective-permute-done((f32[128,1024]{1,0:T(8,128)}, f32[128,1024]{1,0:T(8,128)}, u32[]{:S(2)}, u32[]{:S(2)}) %collective-permute-start.14) | collective-permute-done | bytes 524320 | tf_op jit(solution)/shard_map/source_terms/ppermute | solution.py:14
  83.8 4.9 %collective-permute-done.6 = f32[64,1024]{1,0:T(8,128)S(1)} collective-permute-done((f32[64,1024]{1,0:T(8,128)S(1)}, f32[64,1024]{1,0:T(8,128)S(1)}, u32[]{:S(2)}, u32[]{:S(2)}) %collective-permute-start.6) | collective-permute-done | bytes 262176 | tf_op jit(solution)/shard_map/source_terms/ppermute | solution.py:14
  90.2 7.6 %collective-permute-done.15 = f32[64,1024]{1,0:T(8,128)S(1)} collective-permute-done((f32[64,1024]{1,0:T(8,128)S(1)}, f32[64,1024]{1,0:T(8,128)S(1)}, u32[]{:S(2)}, u32[]{:S(2)}) %collective-permute-start.15) | collective-permute-done | bytes 262176 | tf_op jit(solution)/shard_map/source_terms/ppermute | solution.py:14
  102.3 5.8 %fusion.4 = f32[512,1024]{1,0:T(8,128)S(1)} fusion(f32[512,1024]{1,0:T(8,128)} %constant_dynamic-update-slice_fusion.7, f32[1024,512]{1,0:T(8,128)} %collective-permute-done.9, f32[1024,512]{1,0:T(8,128)S(1)} %get-tuple-element.15), kind=kOutput, calls=%fused_computation.13 | convolution fusion | flops 3222274048 | bytes 8388608 | tf_op jit(solution)/shard_map/source_terms/dot_general | solution.py:42
  108.1 5.8 %fusion.3 = f32[512,1024]{1,0:T(8,128)S(1)} fusion(f32[512,1024]{1,0:T(8,128)} %constant_dynamic-update-slice_fusion.21, f32[1024,512]{1,0:T(8,128)} %collective-permute-done.9, f32[1024,512]{1,0:T(8,128)S(1)} %get-tuple-element.15), kind=kOutput, calls=%fused_computation.12 | convolution fusion | flops 3222274048 | bytes 8388608 | tf_op jit(solution)/shard_map/source_terms/dot_general | solution.py:42
  116.5 8.6 %gather_fusion = f32[1024,1024]{1,0:T(8,128)} fusion(f32[1024,1024]{1,0:T(8,128)} %pad_maximum_fusion.1, s32[1024]{0:T(1024)S(1)} %get-tuple-element.57), kind=kCustom, calls=%fused_computation | custom fusion | bytes 8392704 | tf_op jit(solution)/shard_map/select/gather | solution.py:93
  125.1 9.5 %fusion.2 = f32[1024,1024]{1,0:T(8,128)S(1)} fusion(f32[1024,1024]{1,0:T(8,128)} %all-gather.2.cloned.1.call-done, f32[1024,512]{1,0:T(8,128)} %collective-permute-done.9, f32[1024,512]{1,0:T(8,128)S(1)} %get-tuple-element.15), kind=kOutput, calls=%fused_computation.11 | convolution fusion | flops 6443499520 | bytes 12582912 | tf_op jit(solution)/shard_map/base_terms/dot_general | solution.py:42
  135.3 12.2 %collective-permute-start.18 = (f32[1024,512]{1,0:T(8,128)S(1)}, f32[1024,512]{1,0:T(8,128)S(1)}, u32[]{:S(2)}, u32[]{:S(2)}) collective-permute-start(f32[1024,512]{1,0:T(8,128)S(1)} %slice.133), channel_id=1, source_target_pairs={{8,0},{0,8},{9,1},{1,9},{10,2},{2,10},{11,3},{3,11},{12,4},{4,12},... | collective-permute-start | bytes 6291464 | tf_op jit(solution)/shard_map/reduce_hid/ppermute | solution.py:14
  147.5 3.8 %collective-permute-done.18 = f32[1024,512]{1,0:T(8,128)S(1)} collective-permute-done((f32[1024,512]{1,0:T(8,128)S(1)}, f32[1024,512]{1,0:T(8,128)S(1)}, u32[]{:S(2)}, u32[]{:S(2)}) %collective-permute-start.18) | collective-permute-done | bytes 2097184 | tf_op jit(solution)/shard_map/reduce_hid/ppermute | solution.py:14
  151.7 32.1 %all_to_all.10 = f32[8,128,512]{2,1,0:T(8,128)} all-to-all(f32[8,128,512]{2,1,0:T(8,128)S(1)} %bitcast.5), channel_id=1, replica_groups=mesh['x'=4,'zh'=4,'c'=2,'y'=4,'zl'=2] {'y','zl'}, dimensions={0} | all-to-all | bytes 4194304 | tf_op jit(solution)/shard_map/reduce_hid/all_to_all | solution.py:99
  185.9 28.3 %all_to_all.11 = f32[8,128,512]{2,1,0:T(8,128)} all-to-all(f32[8,128,512]{2,1,0:T(8,128)S(1)} %broadcast_in_dim.9), channel_id=1, replica_groups=mesh['x'=4,'zh'=4,'c'=2,'y'=4,'zl'=2] {'y','zl'}, dimensions={0} | all-to-all | bytes 4194304 | tf_op jit(solution)/shard_map/gather_hid/all_to_all | solution.py:102
  216.9 4.1 %collective-permute-done.19 = f32[1024,512]{1,0:T(8,128)} collective-permute-done((f32[1024,512]{1,0:T(8,128)}, f32[1024,512]{1,0:T(8,128)}, u32[]{:S(2)}, u32[]{:S(2)}) %collective-permute-start.19) | collective-permute-done | bytes 2097184 | tf_op jit(solution)/shard_map/gather_hid/ppermute | solution.py:14
  221.1 7.0 %fusion = f32[1024,384]{1,0:T(8,128)} fusion(f32[1024,512]{1,0:T(8,128)} %collective-permute-done.19, f32[1024,512]{1,0:T(8,128)} %bitcast.1, f32[1024,512]{1,0:T(8,128)S(1)} %get-tuple-element.15, f32[1024,512]{1,0:T(8,128)} %collective-permute-done.9), kind=kOutput, calls=%fused_computation.9 | convolution fusion | flops 2417360896 | bytes 9961472 | tf_op jit(solution)/shard_map/inverse/dot_general | solution.py:42
  228.1 7.4 %fusion.1 = f32[1024,640]{1,0:T(8,128)S(1)} fusion(f32[1024,512]{1,0:T(8,128)} %collective-permute-done.19, f32[1024,512]{1,0:T(8,128)} %bitcast.1, f32[1024,512]{1,0:T(8,128)S(1)} %get-tuple-element.15, f32[1024,512]{1,0:T(8,128)} %collective-permute-done.9), kind=kOutput, calls=%fused_computation.10 | convolution fusion | flops 4028235776 | bytes 11010048 | tf_op jit(solution)/shard_map/inverse/dot_general | solution.py:42
  239.8 8.4 %collective-permute-done.20 = f32[128,640]{1,0:T(8,128)S(1)} collective-permute-done((f32[128,640]{1,0:T(8,128)S(1)}, f32[128,640]{1,0:T(8,128)S(1)}, u32[]{:S(2)}, u32[]{:S(2)}) %collective-permute-start.20) | collective-permute-done | bytes 327712 | tf_op jit(solution)/shard_map/scatter/ppermute | solution.py:14
  252.5 15.3 %collective-permute-done.21 = f32[256,640]{1,0:T(8,128)S(1)} collective-permute-done((f32[256,640]{1,0:T(8,128)S(1)}, f32[256,640]{1,0:T(8,128)S(1)}, u32[]{:S(2)}, u32[]{:S(2)}) %collective-permute-start.21) | collective-permute-done | bytes 655392 | tf_op jit(solution)/shard_map/scatter/ppermute | solution.py:14
  272.9 4.6 %collective-permute-done.24 = f32[32,640]{1,0:T(8,128)S(1)} collective-permute-done((f32[32,640]{1,0:T(8,128)S(1)}, f32[32,640]{1,0:T(8,128)S(1)}, u32[]{:S(2)}, u32[]{:S(2)}) %collective-permute-start.24) | collective-permute-done | bytes 81952 | tf_op jit(solution)/shard_map/scatter/ppermute | solution.py:14
  281.3 4.8 %collective-permute-done.25 = f32[64,640]{1,0:T(8,128)S(1)} collective-permute-done((f32[64,640]{1,0:T(8,128)S(1)}, f32[64,640]{1,0:T(8,128)S(1)}, u32[]{:S(2)}, u32[]{:S(2)}) %collective-permute-start.25) | collective-permute-done | bytes 163872 | tf_op jit(solution)/shard_map/scatter/ppermute | solution.py:14
  286.8 22.8 %reduce-scatter.2.cloned.1.call-done = f32[64,384]{1,0:T(8,128)} async-done(((f32[1024,384]{1,0:T(8,128)}), f32[64,384]{1,0:T(8,128)}) %reduce-scatter.2.cloned.1.call-update) | async-done | bytes 98320 | tf_op jit(solution)/shard_map/scatter/reduce_scatter | solution.py:111
  (113 shorter events, 75.3 us)
Async XLA Ops:
  6.5 118.5 %all-gather.2.cloned.1.call-start = ((), (), s32[]{:S(2)}) async-start(), calls=%async_computation.3 | async-start | bytes 4456448 | tf_op jit(solution)/shard_map/gather_base/all_gather | solution.py:69
  15.3 294.4 %reduce-scatter.2.cloned.1.call-start = ((), (), s32[]{:S(2)}) async-start(), calls=%async_computation.4 | async-start | bytes 1671168 | tf_op jit(solution)/shard_map/scatter/reduce_scatter | solution.py:111
  15.3 13.2 %collective-permute-start.1 = (f32[32,1024]{1,0:T(8,128)S(1)}, f32[32,1024]{1,0:T(8,128)S(1)}, u32[]{:S(2)}, u32[]{:S(2)}) collective-permute-start(f32[32,1024]{1,0:T(8,128)S(1)} %get-tuple-element.36), channel_id=1, source_target_pairs={{16,0},{32,16},{48,32},{0,48},{17,1},{33,17},{49,33},{1,49},{18,2}... | collective-permute-start | bytes 393224 | tf_op jit(solution)/shard_map/source_terms/ppermute | solution.py:14
  19.7 12.8 %collective-permute-start.3 = (f32[32,1024]{1,0:T(8,128)S(1)}, f32[32,1024]{1,0:T(8,128)S(1)}, u32[]{:S(2)}, u32[]{:S(2)}) collective-permute-start(f32[32,1024]{1,0:T(8,128)S(1)} %get-tuple-element.36), channel_id=1, source_target_pairs={{48,0},{0,16},{16,32},{32,48},{49,1},{1,17},{17,33},{33,49},{50,2}... | collective-permute-start | bytes 393224 | tf_op jit(solution)/shard_map/source_terms/ppermute | solution.py:14
  19.7 12.9 %collective-permute-start.10 = (f32[32,1024]{1,0:T(8,128)S(1)}, f32[32,1024]{1,0:T(8,128)S(1)}, u32[]{:S(2)}, u32[]{:S(2)}) collective-permute-start(f32[32,1024]{1,0:T(8,128)S(1)} %get-tuple-element.40), channel_id=1, source_target_pairs={{16,0},{32,16},{48,32},{0,48},{17,1},{33,17},{49,33},{1,49},{18,2}... | collective-permute-start | bytes 393224 | tf_op jit(solution)/shard_map/source_terms/ppermute | solution.py:14
  23.3 12.9 %collective-permute-start.12 = (f32[32,1024]{1,0:T(8,128)S(1)}, f32[32,1024]{1,0:T(8,128)S(1)}, u32[]{:S(2)}, u32[]{:S(2)}) collective-permute-start(f32[32,1024]{1,0:T(8,128)S(1)} %get-tuple-element.40), channel_id=1, source_target_pairs={{48,0},{0,16},{16,32},{32,48},{49,1},{1,17},{17,33},{33,49},{50,2}... | collective-permute-start | bytes 393224 | tf_op jit(solution)/shard_map/source_terms/ppermute | solution.py:14
  27.3 75.0 %collective-permute-start.9 = (f32[1024,512]{1,0:T(8,128)}, f32[1024,512]{1,0:T(8,128)}, u32[]{:S(2)}, u32[]{:S(2)}) collective-permute-start(f32[1024,512]{1,0:T(8,128)} %get-tuple-element.16), channel_id=1, source_target_pairs={{8,0},{0,8},{9,1},{1,9},{10,2},{2,10},{11,3},{3,11},{12,4},{4,12},... | collective-permute-start | bytes 6291464 | tf_op jit(solution)/shard_map/core_swap_in/ppermute | solution.py:14
  28.5 9.1 %collective-permute-start.2 = (f32[16,1024]{1,0:T(8,128)S(1)}, f32[16,1024]{1,0:T(8,128)S(1)}, u32[]{:S(2)}, u32[]{:S(2)}) collective-permute-start(f32[16,1024]{1,0:T(8,128)S(1)} %slice.124), channel_id=1, source_target_pairs={{16,0},{32,16},{48,32},{0,48},{17,1},{33,17},{49,33},{1,49},{18,2}... | collective-permute-start | bytes 196616 | tf_op jit(solution)/shard_map/source_terms/ppermute | solution.py:14
  32.4 9.6 %collective-permute-start.4 = (f32[16,1024]{1,0:T(8,128)S(1)}, f32[16,1024]{1,0:T(8,128)S(1)}, u32[]{:S(2)}, u32[]{:S(2)}) collective-permute-start(f32[16,1024]{1,0:T(8,128)S(1)} %slice.125), channel_id=1, source_target_pairs={{48,0},{0,16},{16,32},{32,48},{49,1},{1,17},{17,33},{33,49},{50,2}... | collective-permute-start | bytes 196616 | tf_op jit(solution)/shard_map/source_terms/ppermute | solution.py:14
  32.6 14.3 %collective-permute-start.11 = (f32[16,1024]{1,0:T(8,128)S(1)}, f32[16,1024]{1,0:T(8,128)S(1)}, u32[]{:S(2)}, u32[]{:S(2)}) collective-permute-start(f32[16,1024]{1,0:T(8,128)S(1)} %slice.128), channel_id=1, source_target_pairs={{16,0},{32,16},{48,32},{0,48},{17,1},{33,17},{49,33},{1,49},{18,2}... | collective-permute-start | bytes 196616 | tf_op jit(solution)/shard_map/source_terms/ppermute | solution.py:14
  36.2 11.4 %collective-permute-start.13 = (f32[16,1024]{1,0:T(8,128)S(1)}, f32[16,1024]{1,0:T(8,128)S(1)}, u32[]{:S(2)}, u32[]{:S(2)}) collective-permute-start(f32[16,1024]{1,0:T(8,128)S(1)} %slice.129), channel_id=1, source_target_pairs={{48,0},{0,16},{16,32},{32,48},{49,1},{1,17},{17,33},{33,49},{50,2}... | collective-permute-start | bytes 196616 | tf_op jit(solution)/shard_map/source_terms/ppermute | solution.py:14
  44.1 14.3 %collective-permute-start.5 = (f32[128,1024]{1,0:T(8,128)}, f32[128,1024]{1,0:T(8,128)S(1)}, u32[]{:S(2)}, u32[]{:S(2)}) collective-permute-start(f32[128,1024]{1,0:T(8,128)} %copy-done.3), channel_id=1, source_target_pairs={{64,0},{128,64},{192,128},{0,192},{65,1},{129,65},{193,129},{1,193... | collective-permute-start | bytes 1572872 | tf_op jit(solution)/shard_map/source_terms/ppermute | solution.py:14
  46.9 13.2 %collective-permute-start.7 = (f32[128,1024]{1,0:T(8,128)}, f32[128,1024]{1,0:T(8,128)S(1)}, u32[]{:S(2)}, u32[]{:S(2)}) collective-permute-start(f32[128,1024]{1,0:T(8,128)} %copy-done.3), channel_id=1, source_target_pairs={{192,0},{0,64},{64,128},{128,192},{193,1},{1,65},{65,129},{129,193... | collective-permute-start | bytes 1572872 | tf_op jit(solution)/shard_map/source_terms/ppermute | solution.py:14
  49.0 28.5 %collective-permute-start.14 = (f32[128,1024]{1,0:T(8,128)}, f32[128,1024]{1,0:T(8,128)}, u32[]{:S(2)}, u32[]{:S(2)}) collective-permute-start(f32[128,1024]{1,0:T(8,128)} %get-tuple-element.45), channel_id=1, source_target_pairs={{64,0},{128,64},{192,128},{0,192},{65,1},{129,65},{193,129},{1,193... | collective-permute-start | bytes 1572872 | tf_op jit(solution)/shard_map/source_terms/ppermute | solution.py:14
  51.7 28.0 %collective-permute-start.16 = (f32[128,1024]{1,0:T(8,128)}, f32[128,1024]{1,0:T(8,128)}, u32[]{:S(2)}, u32[]{:S(2)}) collective-permute-start(f32[128,1024]{1,0:T(8,128)} %get-tuple-element.45), channel_id=1, source_target_pairs={{192,0},{0,64},{64,128},{128,192},{193,1},{1,65},{65,129},{129,193... | collective-permute-start | bytes 1572872 | tf_op jit(solution)/shard_map/source_terms/ppermute | solution.py:14
  58.5 30.2 %collective-permute-start.6 = (f32[64,1024]{1,0:T(8,128)S(1)}, f32[64,1024]{1,0:T(8,128)S(1)}, u32[]{:S(2)}, u32[]{:S(2)}) collective-permute-start(f32[64,1024]{1,0:T(8,128)S(1)} %slice.126), channel_id=1, source_target_pairs={{64,0},{128,64},{192,128},{0,192},{65,1},{129,65},{193,129},{1,193... | collective-permute-start | bytes 786440 | tf_op jit(solution)/shard_map/source_terms/ppermute | solution.py:14
  60.2 29.3 %collective-permute-start.8 = (f32[64,1024]{1,0:T(8,128)S(1)}, f32[64,1024]{1,0:T(8,128)S(1)}, u32[]{:S(2)}, u32[]{:S(2)}) collective-permute-start(f32[64,1024]{1,0:T(8,128)S(1)} %slice.127), channel_id=1, source_target_pairs={{192,0},{0,64},{64,128},{128,192},{193,1},{1,65},{65,129},{129,193... | collective-permute-start | bytes 786440 | tf_op jit(solution)/shard_map/source_terms/ppermute | solution.py:14
  78.5 19.3 %collective-permute-start.15 = (f32[64,1024]{1,0:T(8,128)S(1)}, f32[64,1024]{1,0:T(8,128)S(1)}, u32[]{:S(2)}, u32[]{:S(2)}) collective-permute-start(f32[64,1024]{1,0:T(8,128)S(1)} %slice.130), channel_id=1, source_target_pairs={{64,0},{128,64},{192,128},{0,192},{65,1},{129,65},{193,129},{1,193... | collective-permute-start | bytes 786440 | tf_op jit(solution)/shard_map/source_terms/ppermute | solution.py:14
  80.7 18.1 %collective-permute-start.17 = (f32[64,1024]{1,0:T(8,128)S(1)}, f32[64,1024]{1,0:T(8,128)S(1)}, u32[]{:S(2)}, u32[]{:S(2)}) collective-permute-start(f32[64,1024]{1,0:T(8,128)S(1)} %slice.131), channel_id=1, source_target_pairs={{192,0},{0,64},{64,128},{128,192},{193,1},{1,65},{65,129},{129,193... | collective-permute-start | bytes 786440 | tf_op jit(solution)/shard_map/source_terms/ppermute | solution.py:14
  135.3 16.0 %collective-permute-start.18 = (f32[1024,512]{1,0:T(8,128)S(1)}, f32[1024,512]{1,0:T(8,128)S(1)}, u32[]{:S(2)}, u32[]{:S(2)}) collective-permute-start(f32[1024,512]{1,0:T(8,128)S(1)} %slice.133), channel_id=1, source_target_pairs={{8,0},{0,8},{9,1},{1,9},{10,2},{2,10},{11,3},{3,11},{12,4},{4,12},... | collective-permute-start | bytes 6291464 | tf_op jit(solution)/shard_map/reduce_hid/ppermute | solution.py:14
  237.1 11.1 %collective-permute-start.20 = (f32[128,640]{1,0:T(8,128)S(1)}, f32[128,640]{1,0:T(8,128)S(1)}, u32[]{:S(2)}, u32[]{:S(2)}) collective-permute-start(f32[128,640]{1,0:T(8,128)S(1)} %get-tuple-element.21), channel_id=1, source_target_pairs={{192,0},{0,64},{64,128},{128,192},{193,1},{1,65},{65,129},{129,193... | collective-permute-start | bytes 983048 | tf_op jit(solution)/shard_map/scatter/ppermute | solution.py:14
  237.2 11.0 %collective-permute-start.22 = (f32[128,640]{1,0:T(8,128)S(1)}, f32[128,640]{1,0:T(8,128)S(1)}, u32[]{:S(2)}, u32[]{:S(2)}) collective-permute-start(f32[128,640]{1,0:T(8,128)S(1)} %get-tuple-element.22), channel_id=1, source_target_pairs={{64,0},{128,64},{192,128},{0,192},{65,1},{129,65},{193,129},{1,193... | collective-permute-start | bytes 983048 | tf_op jit(solution)/shard_map/scatter/ppermute | solution.py:14
  249.6 18.2 %collective-permute-start.21 = (f32[256,640]{1,0:T(8,128)S(1)}, f32[256,640]{1,0:T(8,128)S(1)}, u32[]{:S(2)}, u32[]{:S(2)}) collective-permute-start(f32[256,640]{1,0:T(8,128)S(1)} %pad_maximum_fusion.8), channel_id=1, source_target_pairs={{192,0},{0,64},{64,128},{128,192},{193,1},{1,65},{65,129},{129,193... | collective-permute-start | bytes 1966088 | tf_op jit(solution)/shard_map/scatter/ppermute | solution.py:14
  249.8 18.0 %collective-permute-start.23 = (f32[256,640]{1,0:T(8,128)S(1)}, f32[256,640]{1,0:T(8,128)S(1)}, u32[]{:S(2)}, u32[]{:S(2)}) collective-permute-start(f32[256,640]{1,0:T(8,128)S(1)} %pad_maximum_fusion.9), channel_id=1, source_target_pairs={{64,0},{128,64},{192,128},{0,192},{65,1},{129,65},{193,129},{1,193... | collective-permute-start | bytes 1966088 | tf_op jit(solution)/shard_map/scatter/ppermute | solution.py:14
  (13 other events, 130.7 us)
Sparse Core Ops, SparseCore 0:
  15.4 81.9 all-gather.1
  228.2 81.3 reduce-scatter.1
